TPU v7x, 512 devices: a whole 4x8x8 slice. The times are simulated.
512 devices in a mesh: seq: 64 (over y, x, core), tp: 8 (over z).
Axes of the slice: x: 4, y: 8, z: 8, core: 2. Of those that a mesh axis runs over, the one named last changes fastest.
Arguments:
- queries: bfloat16 [32768, 4096], P('seq', 'tp'), may hold values from -9 to 9
- keys: bfloat16 [32768, 4096], P('seq', 'tp'), may hold values from -9 to 9
- values: bfloat16 [32768, 4096], P('seq', 'tp'), may hold values from -6 to 6
- route: int32 [32, 32768], P('tp', 'seq'), may hold values from 0 to 32767, as said below
- members: int32 [32, 32768], P('tp', 'seq'), may hold values from 0 to 32767, as said below
- pattern: int32 [32, 128, 10], P('tp', 'seq'), may hold values from 0 to 1, as said below
- w_out: bfloat16 [4096, 4096], P('tp', 'seq'), may hold values from -0.25 to 0.25
Outputs:
- mixed: bfloat16 [32768, 4096], P('seq', 'tp')
Inputs may be any that keep to these rules, and one draw needn't show every extreme that they name: `route`: each row is a permutation of the positions; for every aligned block of 512 positions and every aligned block of 512 slots, exactly 8 of the block's positions have their slot in that slot block. members[h] is the inverse permutation of route[h]: members[h, route[h, p]] = p. `pattern`: entries 2 * 2 and 2 * 2 + 1 (the cluster's own blocks) are always 1; entries whose cluster lies outside 0 to 127 are always 0.
All inputs are finite; a program needn't handle non-finite values.
Results may differ from a plain program's by a relative error of at most 0.017.
Values may be sent and summed in bfloat16 or wider, within the bound.
A program may use at most 64 MiB of HBM per device.

v0:
```python
import jax
import jax.numpy as jnp
from jax import lax
from jax.sharding import PartitionSpec as P

CLUSTER = 256
REACH = 2


def extended_2(cells, sides, width):
    for axis, dim in sides:
        count = lax.axis_size(axis)
        ends = count - 1
        head = lax.slice_in_dim(cells, 0, width, axis=dim)
        tail = lax.slice_in_dim(cells, cells.shape[dim] - width, cells.shape[dim], axis=dim)
        cells = jnp.concatenate(
            [
                lax.ppermute(tail, axis, [(i, (i + 1) % count) for i in range(ends)]),
                cells,
                lax.ppermute(head, axis, [((i + 1) % count, i) for i in range(ends)]),
            ],
            axis=dim,
        )
    return cells


def attend_head(pieces):
    query_rows, key_rows, value_rows, pattern_rows = pieces
    head_width = query_rows.shape[1]
    cluster_count = query_rows.shape[0] // CLUSTER
    window_rows = (2 * REACH + 1) * CLUSTER
    starts = jnp.arange(cluster_count) * CLUSTER
    key_window = jax.vmap(
        lambda slot_start: lax.dynamic_slice_in_dim(key_rows, slot_start, window_rows, 0)
    )(starts)
    value_window = jax.vmap(
        lambda slot_start: lax.dynamic_slice_in_dim(value_rows, slot_start, window_rows, 0)
    )(starts)
    query_blocks = query_rows.reshape(cluster_count, CLUSTER, head_width)
    scores = jnp.einsum(
        "cqd,ckd->cqk", query_blocks, key_window, preferred_element_type=jnp.float32
    ) * head_width ** (-0.5)
    allowed = jnp.repeat(pattern_rows, CLUSTER // 2, axis=1) > 0
    scores = jnp.where(allowed[:, None, :], scores, -jnp.inf)
    row_max = jnp.max(scores, axis=-1, keepdims=True)
    exponent = jnp.exp(scores - row_max)
    weights = (exponent / jnp.sum(exponent, axis=-1, keepdims=True)).astype(jnp.bfloat16)
    context = jnp.einsum(
        "cqk,ckd->cqd", weights, value_window, preferred_element_type=jnp.float32
    ).astype(jnp.bfloat16)
    return context.reshape(query_rows.shape[0], head_width)


def buffer_index(group_of, order_key, per_peer):
    same_group = group_of[:, :, None] == group_of[:, None, :]
    earlier = order_key[:, None, :] < order_key[:, :, None]
    rank = jnp.sum((same_group & earlier).astype(jnp.int32), axis=2)
    return group_of * per_peer + rank


def shards(queries, keys, values, route, members, pattern, w_out):
    rows_here = queries.shape[0]
    head_count = route.shape[0]
    head_width = queries.shape[1] // head_count
    peer_count = lax.axis_size("seq")
    per_peer = rows_here // peer_count
    local_iota = jnp.arange(rows_here, dtype=jnp.int32)
    send_index = buffer_index(route // rows_here, route, per_peer)
    local_slots = jnp.broadcast_to(local_iota[None, :], members.shape)
    arrival_index = buffer_index(members // rows_here, local_slots, per_peer)
    send_table = (send_index[:, None, :] == local_iota[None, :, None]).astype(jnp.bfloat16)
    land_table = (arrival_index[:, :, None] == local_iota[None, None, :]).astype(jnp.bfloat16)
    stacked = jnp.concatenate(
        [
            queries.reshape(rows_here, head_count, head_width),
            keys.reshape(rows_here, head_count, head_width),
            values.reshape(rows_here, head_count, head_width),
        ],
        axis=2,
    )
    packed = jnp.einsum(
        "hap,phd->had", send_table, stacked, preferred_element_type=jnp.float32
    ).astype(jnp.bfloat16)

    def outgoing(column_index):
        part_rows = packed[:, :, column_index * head_width : (column_index + 1) * head_width]
        return part_rows.reshape(head_count, peer_count, per_peer, head_width)

    sent_query, sent_key, sent_value = (
        lax.all_to_all(outgoing(0), "seq", split_axis=1, concat_axis=1, tiled=True),
        lax.all_to_all(outgoing(1), "seq", split_axis=1, concat_axis=1, tiled=True),
        lax.all_to_all(outgoing(2), "seq", split_axis=1, concat_axis=1, tiled=True),
    )
    arrived = jnp.concatenate(
        [
            sent_query.reshape(head_count, rows_here, head_width),
            sent_key.reshape(head_count, rows_here, head_width),
            sent_value.reshape(head_count, rows_here, head_width),
        ],
        axis=2,
    )
    placed = jnp.einsum(
        "hsa,had->hsd", land_table, arrived, preferred_element_type=jnp.float32
    ).astype(jnp.bfloat16)
    ordered_query = placed[:, :, :head_width]
    keys_values = jnp.stack(
        [placed[:, :, head_width : 2 * head_width], placed[:, :, 2 * head_width :]]
    )
    extended = extended_2(keys_values, (("seq", 2),), REACH * CLUSTER)
    context = lax.map(attend_head, (ordered_query, extended[0], extended[1], pattern))
    returning = jnp.einsum(
        "hsa,hsd->had", land_table, context, preferred_element_type=jnp.float32
    ).astype(jnp.bfloat16)
    returning = returning.reshape(head_count, peer_count, per_peer, head_width)
    returned = lax.all_to_all(returning, "seq", split_axis=1, concat_axis=1, tiled=True).reshape(
        head_count, rows_here, head_width
    )
    attended = jnp.einsum(
        "hap,had->phd", send_table, returned, preferred_element_type=jnp.float32
    ).astype(jnp.bfloat16)
    attended = attended.reshape(rows_here, head_count * head_width)
    partial_value = jnp.dot(
        attended,
        lax.all_gather(w_out, "seq", axis=1, tiled=True),
        preferred_element_type=jnp.float32,
    )
    column_count = partial_value.shape[1] // lax.axis_size("tp")
    summed = lax.psum(partial_value.astype(jnp.bfloat16), "tp").astype(jnp.float32)
    mixed_out = lax.dynamic_slice_in_dim(
        summed, lax.axis_index("tp") * column_count, column_count, 1
    )
    return mixed_out.astype(jnp.bfloat16)


def solution(mesh):
    placed = (
        P("seq", "tp"),
        P("seq", "tp"),
        P("seq", "tp"),
        P("tp", "seq"),
        P("tp", "seq"),
        P("tp", "seq", None),
        P("tp", "seq"),
    )
    return jax.shard_map(
        shards, mesh=mesh, in_specs=placed, out_specs=P("seq", "tp"), check_vma=False
    )
```

profile of v0, /device:TPU:1, one launch (start us, length us, event | category | flops | bytes accessed | tf_op | source)
XLA Modules:
  0.0 320.6 jit_solution(11738363935786757012)
XLA Ops:
  7.3 1.8 convert_reduce_fusion
  16.0 11.6 %all-to-all-start.2 = ((bf16[4,64,8,128]{3,2,0,1:T(8,128)(2,1)}), bf16[4,64,8,128]{3,2,0,1:T(8,128)(2,1)S(1)}, u32[]{:S(2)}, u32[]{:S(2)}) async-start(bf16[4,64,8,128]{3,2,0,1:T(8,128)(2,1)} %copy.44), calls=%async_computation.2 | async-start | bytes 1048576 | tf_op jit(solution)/shard_map/all_to_all | solution.py:92
  28.5 16.8 %all-to-all-done.2 = bf16[4,64,8,128]{3,2,0,1:T(8,128)(2,1)S(1)} async-done(((bf16[4,64,8,128]{3,2,0,1:T(8,128)(2,1)}), bf16[4,64,8,128]{3,2,0,1:T(8,128)(2,1)S(1)}, u32[]{:S(2)}, u32[]{:S(2)}) %all-to-all-start.2) | async-done | bytes 524320 | tf_op jit(solution)/shard_map/all_to_all | solution.py:92
  45.3 5.7 %all-to-all-start.1 = ((bf16[4,64,8,128]{3,2,0,1:T(8,128)(2,1)}), bf16[4,64,8,128]{3,2,0,1:T(8,128)(2,1)S(1)}, u32[]{:S(2)}, u32[]{:S(2)}) async-start(bf16[4,64,8,128]{3,2,0,1:T(8,128)(2,1)} %copy.42), calls=%async_computation.1 | async-start | bytes 1048576 | tf_op jit(solution)/shard_map/all_to_all | solution.py:91
  51.9 16.8 %all-to-all-done.1 = bf16[4,64,8,128]{3,2,0,1:T(8,128)(2,1)S(1)} async-done(((bf16[4,64,8,128]{3,2,0,1:T(8,128)(2,1)}), bf16[4,64,8,128]{3,2,0,1:T(8,128)(2,1)S(1)}, u32[]{:S(2)}, u32[]{:S(2)}) %all-to-all-start.1) | async-done | bytes 524320 | tf_op jit(solution)/shard_map/all_to_all | solution.py:91
  68.8 5.7 %all-to-all-start = ((bf16[4,64,8,128]{3,2,0,1:T(8,128)(2,1)}), bf16[4,64,8,128]{3,2,0,1:T(8,128)(2,1)S(1)}, u32[]{:S(2)}, u32[]{:S(2)}) async-start(bf16[4,64,8,128]{3,2,0,1:T(8,128)(2,1)} %copy.40), calls=%async_computation | async-start | bytes 1048576 | tf_op jit(solution)/shard_map/all_to_all | solution.py:90
  76.1 16.1 %all-to-all-done = bf16[4,64,8,128]{3,2,0,1:T(8,128)(2,1)S(1)} async-done(((bf16[4,64,8,128]{3,2,0,1:T(8,128)(2,1)}), bf16[4,64,8,128]{3,2,0,1:T(8,128)(2,1)S(1)}, u32[]{:S(2)}, u32[]{:S(2)}) %all-to-all-start) | async-done | bytes 524320 | tf_op jit(solution)/shard_map/all_to_all | solution.py:90
  94.9 3.4 %collective-permute-start = (bf16[2,4,512,128]{3,2,1,0:T(8,128)(2,1)S(1)}, bf16[2,4,512,128]{3,2,1,0:T(8,128)(2,1)S(1)}, u32[]{:S(2)}, u32[]{:S(2)}) collective-permute-start(bf16[2,4,512,128]{3,2,1,0:T(8,128)(2,1)S(1)} %pad_maximum_fusion.1), channel_id=1, source_target_pairs={{0,8},{8,16},{16,24},{24,32},{32,40},{40,48},{48,56},{56,64},{64,7... | collective-permute-start | bytes 3145736 | tf_op jit(solution)/shard_map/ppermute | solution.py:18
  98.3 1.9 collective-permute-start.1
  100.5 9.5 %collective-permute-done = bf16[2,4,512,128]{3,2,1,0:T(8,128)(2,1)S(1)} collective-permute-done((bf16[2,4,512,128]{3,2,1,0:T(8,128)(2,1)S(1)}, bf16[2,4,512,128]{3,2,1,0:T(8,128)(2,1)S(1)}, u32[]{:S(2)}, u32[]{:S(2)}) %collective-permute-start) | collective-permute-done | bytes 1048608 | tf_op jit(solution)/shard_map/ppermute | solution.py:18
  110.0 4.5 %collective-permute-done.1 = bf16[2,4,512,128]{3,2,1,0:T(8,128)(2,1)} collective-permute-done((bf16[2,4,512,128]{3,2,1,0:T(8,128)(2,1)S(1)}, bf16[2,4,512,128]{3,2,1,0:T(8,128)(2,1)}, u32[]{:S(2)}, u32[]{:S(2)}) %collective-permute-start.1) | collective-permute-done | bytes 1048608 | tf_op jit(solution)/shard_map/ppermute | solution.py:20
  114.5 1.3 pad_maximum_fusion
  115.8 1.4 slice_bitcast_fusion
  117.2 27.3 %while.16 = (s32[]{:T(128)}, bf16[4,512,128]{2,1,0:T(8,128)(2,1)}, s32[4,2,10]{2,1,0:T(2,128)}, bf16[4,512,128]{2,1,0:T(8,128)(2,1)}, bf16[4,1536,128]{2,1,0:T(8...) while((s32[]{:T(128)}, bf16[4,512,128]{2,1,0:T(8,128)(2,1)}, ...), condition=%wide.region_5.6_spmd, body=%wide.region_2.5_spmd.sunk | while | flops 509283360 | bytes 7096867 | solution.py:110
  122.0 1.4 fusion.66
  128.8 1.4 fusion.66
  135.6 1.4 fusion.66
  142.4 1.4 fusion.66
  144.5 1.8 fusion.35
  146.5 31.2 %all_to_all.20 = bf16[4,64,8,128]{3,2,0,1:T(8,128)(2,1)S(1)} all-to-all(bf16[4,64,8,128]{3,2,0,1:T(8,128)(2,1)S(1)} %copy.47), channel_id=1, replica_groups=mesh['seq'=64,'tp'=8] {'seq'}, dimensions={1} | all-to-all | bytes 1048576 | tf_op jit(solution)/shard_map/all_to_all | solution.py:115
  178.6 11.8 %all-gather.2.cloned.1.call-done = bf16[512,4096]{0,1:T(8,128)(2,1)} async-done(((bf16[512,64]{0,1:T(8,128)(2,1)}), bf16[512,4096]{0,1:T(8,128)(2,1)}) %all-gather.2.cloned.1.call-update) | async-done | bytes 4194320 | tf_op jit(solution)/shard_map/all_gather | solution.py:124
  190.3 6.6 %convolution_convert_fusion = bf16[512,4096]{1,0:T(8,128)(2,1)} fusion(bf16[512,512]{0,1:T(8,128)(2,1)S(1)} %bitcast.112, bf16[512,4096]{0,1:T(8,128)(2,1)} %all-gather.2.cloned.1.call-done), kind=kOutput, calls=%fused_computation.26 | convolution fusion | flops 2149580800 | bytes 8912896 | tf_op jit(solution)/shard_map/dot_general | solution.py:122
  196.9 115.0 %all-reduce.3.cloned.1.call-done = bf16[512,4096]{1,0:T(8,128)(2,1)} async-done(((bf16[512,4096]{1,0:T(8,128)(2,1)}), bf16[512,4096]{1,0:T(8,128)(2,1)}) %all-reduce.3.cloned.1.call-update) | async-done | bytes 4194320 | tf_op jit(solution)/shard_map/psum | solution.py:128
  311.9 1.9 convert_convert_fusion
  (118 shorter events, 39.0 us)
Async XLA Ops:
  6.5 6.4 %copy-start = (bf16[512,512]{1,0:T(8,128)(2,1)S(1)}, bf16[512,512]{1,0:T(8,128)(2,1)}, u32[]{:S(2)}) copy-start(bf16[512,512]{1,0:T(8,128)(2,1)} %param.11) | copy-start | bytes 1572868
  15.1 59.6 %copy-start.1 = (s32[4,512]{1,0:T(4,128)S(1)}, s32[4,512]{1,0:T(4,128)}, u32[]{:S(2)}) copy-start(s32[4,512]{1,0:T(4,128)} %param.13) | copy-start | bytes 24580
  16.0 29.3 %all-to-all-start.2 = ((bf16[4,64,8,128]{3,2,0,1:T(8,128)(2,1)}), bf16[4,64,8,128]{3,2,0,1:T(8,128)(2,1)S(1)}, u32[]{:S(2)}, u32[]{:S(2)}) async-start(bf16[4,64,8,128]{3,2,0,1:T(8,128)(2,1)} %copy.44), calls=%async_computation.2 | async-start | bytes 1048576 | tf_op jit(solution)/shard_map/all_to_all | solution.py:92
  45.3 23.4 %all-to-all-start.1 = ((bf16[4,64,8,128]{3,2,0,1:T(8,128)(2,1)}), bf16[4,64,8,128]{3,2,0,1:T(8,128)(2,1)S(1)}, u32[]{:S(2)}, u32[]{:S(2)}) async-start(bf16[4,64,8,128]{3,2,0,1:T(8,128)(2,1)} %copy.42), calls=%async_computation.1 | async-start | bytes 1048576 | tf_op jit(solution)/shard_map/all_to_all | solution.py:91
  68.8 23.4 %all-to-all-start = ((bf16[4,64,8,128]{3,2,0,1:T(8,128)(2,1)}), bf16[4,64,8,128]{3,2,0,1:T(8,128)(2,1)S(1)}, u32[]{:S(2)}, u32[]{:S(2)}) async-start(bf16[4,64,8,128]{3,2,0,1:T(8,128)(2,1)} %copy.40), calls=%async_computation | async-start | bytes 1048576 | tf_op jit(solution)/shard_map/all_to_all | solution.py:90
  74.5 115.8 %all-gather.2.cloned.1.call-start = ((), (), s32[]{:S(2)}) async-start(), calls=%async_computation.4 | async-start | bytes 4259840 | tf_op jit(solution)/shard_map/all_gather | solution.py:124
  94.9 15.1 %collective-permute-start = (bf16[2,4,512,128]{3,2,1,0:T(8,128)(2,1)S(1)}, bf16[2,4,512,128]{3,2,1,0:T(8,128)(2,1)S(1)}, u32[]{:S(2)}, u32[]{:S(2)}) collective-permute-start(bf16[2,4,512,128]{3,2,1,0:T(8,128)(2,1)S(1)} %pad_maximum_fusion.1), channel_id=1, source_target_pairs={{0,8},{8,16},{16,24},{24,32},{32,40},{40,48},{48,56},{56,64},{64,7... | collective-permute-start | bytes 3145736 | tf_op jit(solution)/shard_map/ppermute | solution.py:18
  98.3 16.2 %collective-permute-start.1 = (bf16[2,4,512,128]{3,2,1,0:T(8,128)(2,1)S(1)}, bf16[2,4,512,128]{3,2,1,0:T(8,128)(2,1)}, u32[]{:S(2)}, u32[]{:S(2)}) collective-permute-start(bf16[2,4,512,128]{3,2,1,0:T(8,128)(2,1)S(1)} %pad_maximum_fusion.1), channel_id=1, source_target_pairs={{8,0},{16,8},{24,16},{32,24},{40,32},{48,40},{56,48},{64,56},{72,6... | collective-permute-start | bytes 3145736 | tf_op jit(solution)/shard_map/ppermute | solution.py:20
  100.2 211.7 %all-reduce.3.cloned.1.call-start = ((), (), s32[]{:S(2)}) async-start(), calls=%async_computation.5 | async-start | bytes 8388608 | tf_op jit(solution)/shard_map/psum | solution.py:128
Sparse Core Ops, SparseCore 0:
  100.3 89.9 all-gather.1
  197.0 114.7 all-reduce.2
where the time goes:
time: 322 us; the launch traced here: 321 us
  waiting for transfers between devices  191 us (59%)
  blocking collectives  31.2 us (10%)
  starting transfers between devices  28.6 us (9%)
  local copies, waits for them, and re-layouts  23.8 us (7%)
  matrix products  21.4 us (7%)
  between operations  13.6 us (4%)
  other arithmetic  10.7 us (3%)
    psum x1, waiting for transfers between devices, shards(): lax.psum(partial_value.astype(jnp.bfloat16), 'tp').astype(jnp.float32)  115 us
    all_to_all x1, blocking collectives, shards(): lax.all_to_all(returning, 'seq', split_axis=1, concat_axis=1, tiled=True)  31.2 us
    all_to_all x1, waiting for transfers between devices, shards(): lax.all_to_all(outgoing(2), 'seq', split_axis=1, concat_axis=1, tiled=True)  16.8 us
    all_to_all x1, waiting for transfers between devices, shards(): lax.all_to_all(outgoing(1), 'seq', split_axis=1, concat_axis=1, tiled=True)  16.8 us
    all_to_all x1, waiting for transfers between devices, shards(): lax.all_to_all(outgoing(0), 'seq', split_axis=1, concat_axis=1, tiled=True)  16.1 us
    all_gather x1, waiting for transfers between devices, shards(): lax.all_gather(w_out, 'seq', axis=1, tiled=True)  11.8 us
    all_to_all x1, starting transfers between devices, shards(): lax.all_to_all(outgoing(2), 'seq', split_axis=1, concat_axis=1, tiled=True)  11.6 us
    ppermute x1, waiting for transfers between devices, extended_2(): lax.ppermute(tail, axis, [(i, (i + 1) % count) for i in range(ends)])  9.53 us
  transfers between devices with their start and end apart: 7, of which 7 were waited for; matrix products, arithmetic and copies ran while one was open for 11% of the time, Pallas kernels for 0%

commit v1 on v0

--- a/solution.py
+++ b/solution.py
@@ -121,7 +121,9 @@
     attended = attended.reshape(rows_here, head_count * head_width)
     partial_value = jnp.dot(
         attended,
-        lax.all_gather(w_out, "seq", axis=1, tiled=True),
+        jnp.concatenate(
+            lax.all_to_all(jnp.stack([w_out] * lax.axis_size("seq")), "seq", 0, 0), axis=1
+        ),
         preferred_element_type=jnp.float32,
     )
     column_count = partial_value.shape[1] // lax.axis_size("tp")

time: 322 us -> 409 us (1.27)
  waiting for transfers between devices: 191 us -> 274 us
  starting transfers between devices: 28.6 us -> 34.5 us
  blocking collectives: 31.2 us -> 26.8 us
    all_to_all x0 -> x1, waiting for transfers between devices: none -> 93.4 us  [shards(): lax.all_to_all(jnp.stack([w_out] * lax.axis_size('seq')), 'seq', 0, 0)]
    all_gather x1 -> x0, waiting for transfers between devices: 11.8 us -> none  [shards(): lax.all_gather(w_out, 'seq', axis=1, tiled=True)]
    all_to_all x0 -> x1, starting transfers between devices: none -> 5.91 us  [shards(): lax.all_to_all(jnp.stack([w_out] * lax.axis_size('seq')), 'seq', 0, 0)]
    all_to_all x1, blocking collectives: 31.2 us -> 26.8 us  [shards(): lax.all_to_all(returning, 'seq', split_axis=1, concat_axis=1, tiled=True)]
  transfers between devices with their start and end apart: 7 -> 7, of which waited for: 7 -> 7; matrix products, arithmetic and copies ran while one was open for 11% -> 1% of each run, Pallas kernels for 0% -> 0%
where the time goes in v1:
time: 409 us; the launch traced here: 408 us
  waiting for transfers between devices  274 us (67%)
  starting transfers between devices  34.5 us (8%)
  blocking collectives  26.8 us (7%)
  local copies, waits for them, and re-layouts  26.2 us (6%)
  matrix products  21.5 us (5%)
  between operations  13.6 us (3%)
  other arithmetic  10.7 us (3%)
    psum x1, waiting for transfers between devices, shards(): lax.psum(partial_value.astype(jnp.bfloat16), 'tp').astype(jnp.float32)  116 us
    all_to_all x1, waiting for transfers between devices, shards(): lax.all_to_all(jnp.stack([w_out] * lax.axis_size('seq')), 'seq', 0, 0)  93.4 us
    all_to_all x1, blocking collectives, shards(): lax.all_to_all(returning, 'seq', split_axis=1, concat_axis=1, tiled=True)  26.8 us
    all_to_all x1, waiting for transfers between devices, shards(): lax.all_to_all(outgoing(2), 'seq', split_axis=1, concat_axis=1, tiled=True)  16.8 us
    all_to_all x1, waiting for transfers between devices, shards(): lax.all_to_all(outgoing(1), 'seq', split_axis=1, concat_axis=1, tiled=True)  16.8 us
    all_to_all x1, waiting for transfers between devices, shards(): lax.all_to_all(outgoing(0), 'seq', split_axis=1, concat_axis=1, tiled=True)  16.1 us
    all_to_all x1, starting transfers between devices, shards(): lax.all_to_all(outgoing(2), 'seq', split_axis=1, concat_axis=1, tiled=True)  11.6 us
    ppermute x1, waiting for transfers between devices, extended_2(): lax.ppermute(tail, axis, [(i, (i + 1) % count) for i in range(ends)])  9.6 us
  transfers between devices with their start and end apart: 7, of which 7 were waited for; matrix products, arithmetic and copies ran while one was open for 1% of the time, Pallas kernels for 0%

profile of v1, /device:TPU:1, one launch (start us, length us, event | category | flops | bytes accessed | tf_op | source)
XLA Modules:
  0.0 407.7 jit_solution(2999723778482218263)
XLA Ops:
  7.3 1.8 convert_reduce_fusion
  15.9 11.6 %all-to-all-start.2 = ((bf16[4,64,8,128]{3,2,0,1:T(8,128)(2,1)}), bf16[4,64,8,128]{3,2,0,1:T(8,128)(2,1)S(1)}, u32[]{:S(2)}, u32[]{:S(2)}) async-start(bf16[4,64,8,128]{3,2,0,1:T(8,128)(2,1)} %copy.45), calls=%async_computation.2 | async-start | bytes 1048576 | tf_op jit(solution)/shard_map/all_to_all | solution.py:92
  28.4 16.8 %all-to-all-done.2 = bf16[4,64,8,128]{3,2,0,1:T(8,128)(2,1)S(1)} async-done(((bf16[4,64,8,128]{3,2,0,1:T(8,128)(2,1)}), bf16[4,64,8,128]{3,2,0,1:T(8,128)(2,1)S(1)}, u32[]{:S(2)}, u32[]{:S(2)}) %all-to-all-start.2) | async-done | bytes 524320 | tf_op jit(solution)/shard_map/all_to_all | solution.py:92
  45.2 5.7 %all-to-all-start.1 = ((bf16[4,64,8,128]{3,2,0,1:T(8,128)(2,1)}), bf16[4,64,8,128]{3,2,0,1:T(8,128)(2,1)S(1)}, u32[]{:S(2)}, u32[]{:S(2)}) async-start(bf16[4,64,8,128]{3,2,0,1:T(8,128)(2,1)} %copy.43), calls=%async_computation.1 | async-start | bytes 1048576 | tf_op jit(solution)/shard_map/all_to_all | solution.py:91
  51.8 16.8 %all-to-all-done.1 = bf16[4,64,8,128]{3,2,0,1:T(8,128)(2,1)S(1)} async-done(((bf16[4,64,8,128]{3,2,0,1:T(8,128)(2,1)}), bf16[4,64,8,128]{3,2,0,1:T(8,128)(2,1)S(1)}, u32[]{:S(2)}, u32[]{:S(2)}) %all-to-all-start.1) | async-done | bytes 524320 | tf_op jit(solution)/shard_map/all_to_all | solution.py:91
  68.7 5.7 %all-to-all-start = ((bf16[4,64,8,128]{3,2,0,1:T(8,128)(2,1)}), bf16[4,64,8,128]{3,2,0,1:T(8,128)(2,1)S(1)}, u32[]{:S(2)}, u32[]{:S(2)}) async-start(bf16[4,64,8,128]{3,2,0,1:T(8,128)(2,1)} %copy.41), calls=%async_computation | async-start | bytes 1048576 | tf_op jit(solution)/shard_map/all_to_all | solution.py:90
  76.0 16.1 %all-to-all-done = bf16[4,64,8,128]{3,2,0,1:T(8,128)(2,1)S(1)} async-done(((bf16[4,64,8,128]{3,2,0,1:T(8,128)(2,1)}), bf16[4,64,8,128]{3,2,0,1:T(8,128)(2,1)S(1)}, u32[]{:S(2)}, u32[]{:S(2)}) %all-to-all-start) | async-done | bytes 524320 | tf_op jit(solution)/shard_map/all_to_all | solution.py:90
  94.8 3.4 collective-permute-start
  98.2 2.1 collective-permute-start.1
  100.3 9.6 %collective-permute-done = bf16[2,4,512,128]{3,2,1,0:T(8,128)(2,1)S(1)} collective-permute-done((bf16[2,4,512,128]{3,2,1,0:T(8,128)(2,1)S(1)}, bf16[2,4,512,128]{3,2,1,0:T(8,128)(2,1)S(1)}, u32[]{:S(2)}, u32[]{:S(2)}) %collective-permute-start) | collective-permute-done | bytes 1048608 | tf_op jit(solution)/shard_map/ppermute | solution.py:18
  109.9 4.5 %collective-permute-done.1 = bf16[2,4,512,128]{3,2,1,0:T(8,128)(2,1)} collective-permute-done((bf16[2,4,512,128]{3,2,1,0:T(8,128)(2,1)S(1)}, bf16[2,4,512,128]{3,2,1,0:T(8,128)(2,1)}, u32[]{:S(2)}, u32[]{:S(2)}) %collective-permute-start.1) | collective-permute-done | bytes 1048608 | tf_op jit(solution)/shard_map/ppermute | solution.py:20
  117.1 27.3 %while.16 = (s32[]{:T(128)}, bf16[4,512,128]{2,1,0:T(8,128)(2,1)}, s32[4,2,10]{2,1,0:T(2,128)}, bf16[4,512,128]{2,1,0:T(8,128)(2,1)}, bf16[4,1536,128]{2,1,0:T(8...) while((s32[]{:T(128)}, bf16[4,512,128]{2,1,0:T(8,128)(2,1)}, ...), condition=%wide.region_5.6_spmd, body=%wide.region_2.5_spmd.sunk | while | flops 509283360 | bytes 7096867 | solution.py:110
  121.8 1.4 fusion.66
  128.7 1.4 fusion.66
  135.5 1.4 fusion.66
  142.3 1.4 fusion.66
  144.4 1.9 fusion.35
  146.4 26.8 %all_to_all.25 = bf16[4,64,8,128]{3,2,0,1:T(8,128)(2,1)S(1)} all-to-all(bf16[4,64,8,128]{3,2,0,1:T(8,128)(2,1)S(1)} %copy.48), channel_id=1, replica_groups=mesh['seq'=64,'tp'=8] {'seq'}, dimensions={1} | all-to-all | bytes 1048576 | tf_op jit(solution)/shard_map/all_to_all | solution.py:115
  173.1 2.5 stack.11
  175.6 5.9 %all-to-all-start.4 = ((bf16[64,512,64]{1,2,0:T(8,128)(2,1)}), bf16[64,512,64]{1,2,0:T(8,128)(2,1)}, u32[]{:S(2)}, u32[]{:S(2)}) async-start(bf16[64,512,64]{1,2,0:T(8,128)(2,1)} %stack.11), calls=%async_computation.4 | async-start | bytes 8388608 | tf_op jit(solution)/shard_map/all_to_all | solution.py:125
  182.5 93.4 %all-to-all-done.4 = bf16[64,512,64]{1,2,0:T(8,128)(2,1)} async-done(((bf16[64,512,64]{1,2,0:T(8,128)(2,1)}), bf16[64,512,64]{1,2,0:T(8,128)(2,1)}, u32[]{:S(2)}, u32[]{:S(2)}) %all-to-all-start.4) | async-done | bytes 4194336 | tf_op jit(solution)/shard_map/all_to_all | solution.py:125
  276.0 6.6 %convolution_convert_fusion = bf16[512,4096]{1,0:T(8,128)(2,1)} fusion(bf16[512,512]{0,1:T(8,128)(2,1)S(1)} %bitcast.115, bf16[512,4096]{0,1:T(8,128)(2,1)} %bitcast.23), kind=kOutput, calls=%fused_computation.26 | convolution fusion | flops 2149580800 | bytes 8912896 | tf_op jit(solution)/shard_map/dot_general | solution.py:122
  282.6 116.5 %all-reduce.3.cloned.1.call-done = bf16[512,4096]{1,0:T(8,128)(2,1)} async-done(((bf16[512,4096]{1,0:T(8,128)(2,1)}), bf16[512,4096]{1,0:T(8,128)(2,1)}) %all-reduce.3.cloned.1.call-update) | async-done | bytes 4194320 | tf_op jit(solution)/shard_map/psum | solution.py:130
  399.0 1.9 convert_convert_fusion
  (120 shorter events, 41.3 us)
Async XLA Ops:
  6.5 6.4 %copy-start = (bf16[512,512]{1,0:T(8,128)(2,1)S(1)}, bf16[512,512]{1,0:T(8,128)(2,1)}, u32[]{:S(2)}) copy-start(bf16[512,512]{1,0:T(8,128)(2,1)} %param.11) | copy-start | bytes 1572868
  15.0 59.5 %copy-start.2 = (s32[4,512]{1,0:T(4,128)S(1)}, s32[4,512]{1,0:T(4,128)}, u32[]{:S(2)}) copy-start(s32[4,512]{1,0:T(4,128)} %param.13) | copy-start | bytes 24580
  15.9 29.3 %all-to-all-start.2 = ((bf16[4,64,8,128]{3,2,0,1:T(8,128)(2,1)}), bf16[4,64,8,128]{3,2,0,1:T(8,128)(2,1)S(1)}, u32[]{:S(2)}, u32[]{:S(2)}) async-start(bf16[4,64,8,128]{3,2,0,1:T(8,128)(2,1)} %copy.45), calls=%async_computation.2 | async-start | bytes 1048576 | tf_op jit(solution)/shard_map/all_to_all | solution.py:92
  45.2 23.4 %all-to-all-start.1 = ((bf16[4,64,8,128]{3,2,0,1:T(8,128)(2,1)}), bf16[4,64,8,128]{3,2,0,1:T(8,128)(2,1)S(1)}, u32[]{:S(2)}, u32[]{:S(2)}) async-start(bf16[4,64,8,128]{3,2,0,1:T(8,128)(2,1)} %copy.43), calls=%async_computation.1 | async-start | bytes 1048576 | tf_op jit(solution)/shard_map/all_to_all | solution.py:91
  68.7 23.4 %all-to-all-start = ((bf16[4,64,8,128]{3,2,0,1:T(8,128)(2,1)}), bf16[4,64,8,128]{3,2,0,1:T(8,128)(2,1)S(1)}, u32[]{:S(2)}, u32[]{:S(2)}) async-start(bf16[4,64,8,128]{3,2,0,1:T(8,128)(2,1)} %copy.41), calls=%async_computation | async-start | bytes 1048576 | tf_op jit(solution)/shard_map/all_to_all | solution.py:90
  94.8 15.1 %collective-permute-start = (bf16[2,4,512,128]{3,2,1,0:T(8,128)(2,1)S(1)}, bf16[2,4,512,128]{3,2,1,0:T(8,128)(2,1)S(1)}, u32[]{:S(2)}, u32[]{:S(2)}) collective-permute-start(bf16[2,4,512,128]{3,2,1,0:T(8,128)(2,1)S(1)} %pad_maximum_fusion.1), channel_id=1, source_target_pairs={{0,8},{8,16},{16,24},{24,32},{32,40},{40,48},{48,56},{56,64},{64,7... | collective-permute-start | bytes 3145736 | tf_op jit(solution)/shard_map/ppermute | solution.py:18
  98.2 16.2 %collective-permute-start.1 = (bf16[2,4,512,128]{3,2,1,0:T(8,128)(2,1)S(1)}, bf16[2,4,512,128]{3,2,1,0:T(8,128)(2,1)}, u32[]{:S(2)}, u32[]{:S(2)}) collective-permute-start(bf16[2,4,512,128]{3,2,1,0:T(8,128)(2,1)S(1)} %pad_maximum_fusion.1), channel_id=1, source_target_pairs={{8,0},{16,8},{24,16},{32,24},{40,32},{48,40},{56,48},{64,56},{72,6... | collective-permute-start | bytes 3145736 | tf_op jit(solution)/shard_map/ppermute | solution.py:20
  144.4 28.8 %copy-start.1 = (bf16[512,64]{0,1:T(8,128)(2,1)S(1)}, bf16[512,64]{0,1:T(8,128)(2,1)}, u32[]{:S(2)}) copy-start(bf16[512,64]{0,1:T(8,128)(2,1)} %param.15) | copy-start | bytes 196612
  175.6 100.3 %all-to-all-start.4 = ((bf16[64,512,64]{1,2,0:T(8,128)(2,1)}), bf16[64,512,64]{1,2,0:T(8,128)(2,1)}, u32[]{:S(2)}, u32[]{:S(2)}) async-start(bf16[64,512,64]{1,2,0:T(8,128)(2,1)} %stack.11), calls=%async_computation.4 | async-start | bytes 8388608 | tf_op jit(solution)/shard_map/all_to_all | solution.py:125
  181.5 217.5 %all-reduce.3.cloned.1.call-start = ((), (), s32[]{:S(2)}) async-start(), calls=%async_computation.5 | async-start | bytes 8388608 | tf_op jit(solution)/shard_map/psum | solution.py:130
Sparse Core Ops, SparseCore 0:
  282.7 116.3 all-reduce.2
